TPU v7x, 32 devices: a whole 2x2x4 slice. The times are simulated.
32 devices in a mesh: gx: 8 (over y, x, core), gy: 4 (over z).
Axes of the slice: x: 2, y: 2, z: 4, core: 2. Of those that a mesh axis runs over, the one named last changes fastest.
Arguments:
- state: float32 [4, 64, 128, 512], P(None, None, 'gx', 'gy'), may hold values from -6 to 6
- damping: float32 [4, 64], replicated, may hold values from 0.02 to 0.2
- k_longwave: float32 [8, 4], replicated, may hold values from 0.02 to 0.2
- k_shortwave: float32 [8, 4], replicated, may hold values from 0.02 to 0.2
- solar: float32 [8], replicated, may hold values from 2 to 8
- daylight: int32 [4, 128], P('gy'), may hold values from 0 to 1, as said below
- cloud_top: int32 [4, 128], P('gy'), may hold values from 0 to 64
Outputs:
- updated: float32 [4, 64, 128, 512], P(None, None, 'gx', 'gy')
Inputs may be any that keep to these rules, and one draw needn't show every extreme that they name: daylight is the same on the 16 rows of one gx index; in each column tile, the gx indices g and g + 8 / 2 (modulo 8) have opposite daylight.
All inputs are finite; a program needn't handle non-finite values.
Results may differ from a plain program's by a relative error of at most 0.0003.
Values sent between devices are 32-bit elements; how exact they have to be, the bound alone decides.
A program may use at most 128 MiB of HBM per device.

v0:
```python
import math

import jax
import numpy as np
import jax.numpy as jnp
from jax import lax
from jax.experimental import pallas as pl
from jax.experimental.pallas import tpu as pltpu
from jax.sharding import PartitionSpec as P

time_step = 0.1
F32 = jnp.float32
BF16 = jnp.bfloat16
LOG2E = math.log2(math.e)
PARTS = 14


def split(value):
    high = value.astype(BF16)
    low = (value - high.astype(F32)).astype(BF16)
    return high, low


def build_mixing(mix, k_ref, first, cloud_depth, rows):
    bands = k_ref.shape[0]
    width = mix.shape[1]
    group = lax.broadcasted_iota(jnp.int32, (bands, width), 1) // rows
    k_high, k_low = split(k_ref[...])
    k_high, k_low = k_high.astype(F32), k_low.astype(F32)
    cloud_high = float(np.asarray(cloud_depth, dtype=BF16))
    spread = jnp.where(group == 12, cloud_high, jnp.where(group == 13, cloud_depth - cloud_high, 0.0))
    for field in range(4):
        high = jnp.broadcast_to(k_high[:, field : field + 1], (bands, width))
        low = jnp.broadcast_to(k_low[:, field : field + 1], (bands, width))
        spread = jnp.where((group == field) | (group == field + 8), high, spread)
        spread = jnp.where(group == field + 4, low, spread)
    lane = lax.broadcasted_iota(jnp.int32, (rows, width), 1)
    row = lax.broadcasted_iota(jnp.int32, (rows, width), 0)
    own = lane % rows == row
    for band in range(bands):
        block = jnp.broadcast_to(spread[band : band + 1], (rows, width))
        mix[(first + band) * rows : (first + band + 1) * rows] = jnp.where(own, block, 0.0).astype(BF16)


def kernel(
    damping, solar, state, north, south, sides, k_lw, k_sw, daylight, cloud_top, out,
    mix, emit, depth, factors, values,
):
    fields, levels, rows, cols = state.shape
    lwb, swb = k_lw.shape[0], k_sw.shape[0]
    bands = lwb + swb
    half = 8
    me = lax.axis_index("gx")

    build_mixing(mix, k_lw, 0, 0.5, rows)
    build_mixing(mix, k_sw, lwb, 0.3, rows)

    lane = lax.broadcasted_iota(jnp.int32, (rows, cols), 1)
    row = lax.broadcasted_iota(jnp.int32, (rows, cols), 0)
    total = cloud_top.shape[1]
    wide_lane = lax.broadcasted_iota(jnp.int32, (rows, total), 1)
    wide_row = lax.broadcasted_iota(jnp.int32, (rows, total), 0)
    mine = wide_lane == me * rows + wide_row
    tops = jnp.sum(jnp.where(mine, cloud_top[...].astype(F32), 0.0), axis=1, keepdims=True)
    tops = jnp.broadcast_to(tops, (rows, cols)).astype(jnp.int32)
    days = jnp.sum(jnp.where(mine, daylight[...].astype(F32), 0.0), axis=1, keepdims=True)
    days = time_step * jnp.broadcast_to(days, (rows, cols))

    def damp_level(level):
        cloudy = jnp.where(level >= tops, 1.0, 0.0).astype(F32)
        highs, lows = [], []
        for field in range(fields):
            centre = state[field, level]
            up = jnp.where(row == 0, north[field, pl.ds(level, 1)], pltpu.roll(centre, 1, 0))
            down = jnp.where(row == rows - 1, south[field, pl.ds(level, 1)], pltpu.roll(centre, rows - 1, 0))
            side = pltpu.roll(sides[field], lax.rem(cols - 2 * level, cols), 1)
            left = jnp.where(lane == 0, side, pltpu.roll(centre, 1, 1))
            right = jnp.where(lane == cols - 1, side, pltpu.roll(centre, cols - 1, 1))
            laplace = (up + down) + (left + right) - 4.0 * centre
            damped = centre + damping[field, level] * laplace
            if field == 0:
                emit[level] = jnp.exp(0.3 * jnp.tanh(damped))
            if field == 1:
                out[field, level] = damped - (2.0 * time_step) * cloudy * damped
            else:
                out[field, level] = damped
            high, low = split(damped * damped)
            highs.append(high)
            lows.append(low)
        cloud = cloudy.astype(BF16)
        return jnp.concatenate(highs + highs + lows + [cloud, cloud], 0)

    @pl.loop(0, levels // 2)
    def _(pair):
        operand = jnp.concatenate([damp_level(2 * pair), damp_level(2 * pair + 1)], 1)
        result = jnp.dot(mix[...], operand, preferred_element_type=F32)
        depth[2 * pair] = result[:, :cols]
        depth[2 * pair + 1] = result[:, cols:]

    zero = jnp.zeros((half, cols), F32)
    log20 = math.log2(20.0)

    for part in range(rows // half):
        at = [band * rows + part * half for band in range(bands)]
        here = slice(part * half, (part + 1) * half)

        def forward(level, carry):
            carry = list(carry)
            emission = emit[level, here]
            last = jnp.where(level == levels - 1, 0.0, 1.0).astype(F32)
            for band in range(bands):
                g, h = carry[2 * band], carry[2 * band + 1]
                d = depth[level, at[band] : at[band] + half]
                coupling = last * jnp.exp2(log20 - (0.1 * LOG2E) * d)
                if band < lwb:
                    source = d * emission
                else:
                    source = solar[band - lwb] * (1.0 - jnp.exp2(-LOG2E * d))
                q = (1.0 + d) + g
                w = source + h
                r = pl.reciprocal(q + coupling, approx=True)
                factor = coupling * r
                factors[level, at[band] : at[band] + half] = factor
                values[level, at[band] : at[band] + half] = w * r
                carry[2 * band], carry[2 * band + 1] = factor * q, factor * w
            return tuple(carry)

        lax.fori_loop(0, levels, forward, (zero,) * (2 * bands))

        def backward(step, carry):
            carry = list(carry)
            level = levels - 1 - step
            emission = emit[level, here]
            lw, sw = zero, zero
            for band in range(bands):
                d = depth[level, at[band] : at[band] + half]
                x = (
                    values[level, at[band] : at[band] + half]
                    + factors[level, at[band] : at[band] + half] * carry[band]
                )
                carry[band] = x
                if band < lwb:
                    lw = lw + d * (x - emission)
                else:
                    sw = sw + d * x
            out[0, level, here] = out[0, level, here] + (time_step * lw + days[here] * sw)
            return tuple(carry)

        lax.fori_loop(0, levels, backward, (zero,) * bands)


def shards(state, damping, k_longwave, k_shortwave, solar, daylight, cloud_top):
    fields, levels, rows, cols = state.shape
    bands = k_longwave.shape[0] + k_shortwave.shape[0]

    def ring(axis, step):
        count = lax.axis_size(axis)
        return [(i, (i + step) % count) for i in range(count)]

    north = lax.ppermute(state[:, :, rows - 1], "gx", ring("gx", 1))
    south = lax.ppermute(state[:, :, 0], "gx", ring("gx", -1))
    west = lax.ppermute(jnp.swapaxes(state[:, :, :, cols - 1], 1, 2), "gy", ring("gy", 1))
    east = lax.ppermute(jnp.swapaxes(state[:, :, :, 0], 1, 2), "gy", ring("gy", -1))
    sides = jnp.stack([west, jnp.roll(east, -1, 2)], 3).reshape(fields, rows, 2 * levels)
    vmem = pl.BlockSpec(memory_space=pltpu.VMEM)
    smem = pl.BlockSpec(memory_space=pltpu.SMEM)
    return pl.pallas_call(
        kernel,
        out_shape=jax.ShapeDtypeStruct(state.shape, F32),
        in_specs=[smem, smem] + [vmem] * 8,
        out_specs=vmem,
        scratch_shapes=[
            pltpu.VMEM((bands * rows, PARTS * rows), BF16),
            pltpu.VMEM((levels, rows, cols), F32),
            pltpu.VMEM((levels, bands * rows, cols), F32),
            pltpu.VMEM((levels, bands * rows, cols), F32),
            pltpu.VMEM((levels, bands * rows, cols), F32),
        ],
        compiler_params=pltpu.CompilerParams(vmem_limit_bytes=48 * 1024 * 1024),
        cost_estimate=pl.CostEstimate(flops=100_000_000, bytes_accessed=4_000_000, transcendentals=5_000_000),
    )(damping, solar, state, north, south, sides, k_longwave, k_shortwave, daylight, cloud_top)


def solution(mesh):
    in_specs = (P(None, None, "gx", "gy"), P(), P(), P(), P(), P("gy", None), P("gy", None))
    out_specs = P(None, None, "gx", "gy")
    return jax.shard_map(shards, mesh=mesh, in_specs=in_specs, out_specs=out_specs, check_vma=False)
```

profile of v0, /device:TPU:0, one launch (start us, length us, event | category | flops | bytes accessed | tf_op | source)
XLA Modules:
  0.0 42.1 jit_solution(10390557827224092793)
XLA Ops:
  0.0 4.9 %fusion = (f32[4,64,16,1]{3,2,1,0:T(8,128)}, f32[4,64,16,1]{3,2,1,0:T(8,128)}) fusion(f32[4,64,16,128]{3,2,1,0:T(8,128)} %state.1), kind=kLoop, calls=%fused_computation.2 | loop fusion | bytes 65536 | tf_op jit(solution)/shard_map/slice | solution.py:162
  4.9 2.5 %copy.25 = f32[4,64,16,1]{1,2,0,3:T(8,128)S(1)} copy(f32[4,64,16,1]{3,2,1,0:T(8,128)} %get-tuple-element.6) | data formatting | bytes 32768
  7.5 5.1 %collective-permute-start.3 = (f32[4,16,64]{2,1,0:T(8,128)S(1)}, f32[4,16,64]{2,1,0:T(8,128)S(1)}, u32[]{:S(2)}, u32[]{:S(2)}) collective-permute-start(f32[4,16,64]{2,1,0:T(8,128)S(1)} %bitcast.22), channel_id=1, source_target_pairs={{0,3},{1,0},{2,1},{3,2},{4,7},{5,4},{6,5},{7,6},{8,11},{9,8},{10,9... | collective-permute-start | bytes 49160 | tf_op jit(solution)/shard_map/ppermute | solution.py:163
  12.6 2.4 %copy.24 = f32[4,64,16,1]{1,2,3,0:T(8,128)S(1)} copy(f32[4,64,16,1]{3,2,1,0:T(8,128)} %get-tuple-element.5) | data formatting | bytes 32768
  14.9 0.0 collective-permute-start.2
  15.0 0.0 copy-done
  15.0 0.2 fusion.1
  15.2 0.1 collective-permute-start
  15.2 2.6 %collective-permute-start.1 = (f32[4,64,128]{2,1,0:T(8,128)S(1)}, f32[4,64,128]{2,1,0:T(8,128)S(1)}, u32[]{:S(2)}, u32[]{:S(2)}) collective-permute-start(f32[4,64,128]{2,1,0:T(8,128)S(1)} %bitcast.19), channel_id=1, source_target_pairs={{0,28},{4,0},{8,4},{12,8},{16,12},{20,16},{24,20},{28,24},{1,29},{... | collective-permute-start | bytes 393224 | tf_op jit(solution)/shard_map/ppermute | solution.py:161
  17.9 0.0 copy-done.5
  17.9 0.1 copy.20.k_lw
  18.0 0.0 copy-done.6
  18.0 0.1 copy.21.k_sw
  18.0 0.0 collective-permute-done.3
  18.0 0.1 slice.26
  18.1 0.1 maximum_bitcast_fusion
  18.2 2.5 %collective-permute-done.2 = f32[4,16,64]{2,1,0:T(8,128)S(1)} collective-permute-done((f32[4,16,64]{2,1,0:T(8,128)S(1)}, f32[4,16,64]{2,1,0:T(8,128)S(1)}, u32[]{:S(2)}, u32[]{:S(2)}) %collective-permute-start.2) | collective-permute-done | bytes 16416 | tf_op jit(solution)/shard_map/ppermute | solution.py:162
  20.7 0.2 copy.18
  20.8 0.1 copy.19.sides
  20.9 0.0 collective-permute-done.north
  20.9 0.0 collective-permute-done.1.south
  21.0 0.0 copy-done.1
  21.0 0.0 copy-done.2
  21.0 21.1 %shard_map.73 = f32[4,64,16,128]{3,2,1,0:T(8,128)} custom-call(f32[4,64]{1,0:T(4,128)S(1)} %copy-done.1, f32[8]{0:T(128)S(1)} %copy-done.2, f32[4,64,16,128]{3,2,1,0:T(8,128)S(1)} %copy-done, f32[4,64,128]{2,1,0:T(8,128)S(1)} %collective-permute-done.north, f32[4,64,128]{2,1,0:T(8,128)S(1)} %collective-permute-done.1.south, f32[4,16,128]{2,1,0:T(8,128)S(1)} %copy.19.sides, ...), custom_call_target="tpu_custom_call" | custom-call | flops 100000000 | bytes 4000000 | tf_op jit(solution)/shard_map/pallas_call | solution.py:167
  (10 shorter events, 0.0 us)
Async XLA Ops:
  4.9 10.1 %copy-start = (f32[4,64,16,128]{3,2,1,0:T(8,128)S(1)}, f32[4,64,16,128]{3,2,1,0:T(8,128)}, u32[]{:S(2)}) copy-start(f32[4,64,16,128]{3,2,1,0:T(8,128)} %state.1) | copy-start | bytes 6291460
  4.9 13.0 %copy-start.5 = (f32[8,4]{0,1:T(4,128)S(1)}, f32[8,4]{0,1:T(4,128)}, u32[]{:S(2)}) copy-start(f32[8,4]{0,1:T(4,128)} %param.9) | copy-start | bytes 388
  4.9 13.0 %copy-start.6 = (f32[8,4]{0,1:T(4,128)S(1)}, f32[8,4]{0,1:T(4,128)}, u32[]{:S(2)}) copy-start(f32[8,4]{0,1:T(4,128)} %param.10) | copy-start | bytes 388
  7.4 13.5 %copy-start.1 = (f32[4,64]{1,0:T(4,128)S(1)}, f32[4,64]{1,0:T(4,128)}, u32[]{:S(2)}) copy-start(f32[4,64]{1,0:T(4,128)} %damping.1) | copy-start | bytes 3076
  7.4 13.5 %copy-start.2 = (f32[8]{0:T(128)S(1)}, f32[8]{0:T(128)}, u32[]{:S(2)}) copy-start(f32[8]{0:T(128)} %solar.1) | copy-start | bytes 100
  7.5 13.5 %copy-start.3 = (s32[1,128]{1,0:T(1,128)S(1)}, s32[1,128]{1,0:T(1,128)}, u32[]{:S(2)}) copy-start(s32[1,128]{1,0:T(1,128)} %daylight.1) | copy-start | bytes 1540
  7.5 13.5 %copy-start.4 = (s32[1,128]{1,0:T(1,128)S(1)}, s32[1,128]{1,0:T(1,128)}, u32[]{:S(2)}) copy-start(s32[1,128]{1,0:T(1,128)} %cloud_top.1) | copy-start | bytes 1540
  7.5 10.6 %collective-permute-start.3 = (f32[4,16,64]{2,1,0:T(8,128)S(1)}, f32[4,16,64]{2,1,0:T(8,128)S(1)}, u32[]{:S(2)}, u32[]{:S(2)}) collective-permute-start(f32[4,16,64]{2,1,0:T(8,128)S(1)} %bitcast.22), channel_id=1, source_target_pairs={{0,3},{1,0},{2,1},{3,2},{4,7},{5,4},{6,5},{7,6},{8,11},{9,8},{10,9... | collective-permute-start | bytes 49160 | tf_op jit(solution)/shard_map/ppermute | solution.py:163
  14.9 5.7 %collective-permute-start.2 = (f32[4,16,64]{2,1,0:T(8,128)S(1)}, f32[4,16,64]{2,1,0:T(8,128)S(1)}, u32[]{:S(2)}, u32[]{:S(2)}) collective-permute-start(f32[4,16,64]{2,1,0:T(8,128)S(1)} %bitcast.21), channel_id=1, source_target_pairs={{0,1},{1,2},{2,3},{3,0},{4,5},{5,6},{6,7},{7,4},{8,9},{9,10},{10,1... | collective-permute-start | bytes 49160 | tf_op jit(solution)/shard_map/ppermute | solution.py:162
  15.2 5.8 %collective-permute-start = (f32[4,64,128]{2,1,0:T(8,128)S(1)}, f32[4,64,128]{2,1,0:T(8,128)S(1)}, u32[]{:S(2)}, u32[]{:S(2)}) collective-permute-start(f32[4,64,128]{2,1,0:T(8,128)S(1)} %bitcast.20), channel_id=1, source_target_pairs={{0,4},{4,8},{8,12},{12,16},{16,20},{20,24},{24,28},{28,0},{1,5},{5... | collective-permute-start | bytes 393224 | tf_op jit(solution)/shard_map/ppermute | solution.py:160
  15.2 5.7 %collective-permute-start.1 = (f32[4,64,128]{2,1,0:T(8,128)S(1)}, f32[4,64,128]{2,1,0:T(8,128)S(1)}, u32[]{:S(2)}, u32[]{:S(2)}) collective-permute-start(f32[4,64,128]{2,1,0:T(8,128)S(1)} %bitcast.19), channel_id=1, source_target_pairs={{0,28},{4,0},{8,4},{12,8},{16,12},{20,16},{24,20},{28,24},{1,29},{... | collective-permute-start | bytes 393224 | tf_op jit(solution)/shard_map/ppermute | solution.py:161
where the time goes:
time: 42.6 us; the launch traced here: 42.1 us
  Pallas kernels  21.1 us (50%)
  local copies, waits for them, and re-layouts  10.5 us (25%)
  starting transfers between devices  7.81 us (18%)
  waiting for transfers between devices  2.48 us (6%)
    pallas_call x1, Pallas kernels, shards(): pl.pallas_call(kernel, out_shape=jax.ShapeDtypeStruct(state.shape, F32),...  21.1 us
    ppermute x1, starting transfers between devices, shards(): lax.ppermute(jnp.swapaxes(state[:, :, :, 0], 1, 2), 'gy', ring('gy', -1))  5.1 us
    unnamed x18, local copies, waits for them, and re-layouts  5.09 us
    slice x1, local copies, waits for them, and re-layouts, shards(): state[:, :, :, cols - 1]  4.91 us
    ppermute x1, starting transfers between devices, shards(): south = lax.ppermute(state[:, :, 0], 'gx', ring('gx', -1))  2.63 us
    ppermute x1, waiting for transfers between devices, shards(): lax.ppermute(jnp.swapaxes(state[:, :, :, cols - 1], 1, 2), 'gy', ring('gy...  2.48 us
  transfers between devices with their start and end apart: 4, of which 1 were waited for; matrix products, arithmetic and copies ran while one was open for 7% of the time, Pallas kernels for 0%

commit v1 on v0

--- a/solution.py
+++ b/solution.py
@@ -1,3 +1,4 @@
+import functools
 import math
 
 import jax
@@ -13,6 +14,9 @@
 BF16 = jnp.bfloat16
 LOG2E = math.log2(math.e)
 PARTS = 14
+
+
+PAIRS, AHEAD, BACK = 2, 4, 4
 
 
 def split(value):
@@ -42,9 +46,59 @@
         mix[(first + band) * rows : (first + band + 1) * rows] = jnp.where(own, block, 0.0).astype(BF16)
 
 
+def exchange(shape, state, north, south, west, east, first, final, packed, send, recv):
+    n_gx, n_gy = shape
+    fields, levels, rows, cols = state.shape
+    gx, gy = lax.axis_index("gx"), lax.axis_index("gy")
+    after, before = lax.rem(gx + 1, n_gx), lax.rem(gx + n_gx - 1, n_gx)
+    right, left = lax.rem(gy + 1, n_gy), lax.rem(gy + n_gy - 1, n_gy)
+    peers = ({"gx": after}, {"gx": before}, {"gy": right}, {"gy": left})
+
+    barrier = pltpu.get_barrier_semaphore()
+    for peer in peers:
+        pl.semaphore_signal(barrier, inc=1, device_id=peer, device_id_type=pl.DeviceIdType.MESH)
+    for field in range(fields):
+        first[field] = state[field, :, 0, :]
+        final[field] = state[field, :, rows - 1, :]
+    pl.semaphore_wait(barrier, 4)
+
+    moves = ((final, north), (first, south), (packed, west), (packed, east))
+    copies = [
+        pltpu.make_async_remote_copy(
+            src_ref=source,
+            dst_ref=target,
+            send_sem=send.at[index],
+            recv_sem=recv.at[index],
+            device_id=peers[index],
+            device_id_type=pl.DeviceIdType.MESH,
+        )
+        for index, (source, target) in enumerate(moves)
+    ]
+    copies[0].start()
+    copies[1].start()
+    pair = lax.broadcasted_iota(jnp.int32, (rows, cols), 1) // 2
+
+    def pack(step, held):
+        held = list(held)
+        for inner in range(8):
+            level = 8 * step + inner
+            for field in range(fields):
+                turned = pltpu.roll(state[field, level], 2 * level + 1, 1)
+                held[field] = jnp.where(pair == level, turned, held[field])
+        return tuple(held)
+
+    held = lax.fori_loop(0, levels // 8, pack, (jnp.zeros((rows, cols), F32),) * fields)
+    for field in range(fields):
+        packed[field] = held[field]
+    copies[2].start()
+    copies[3].start()
+    for copy in copies:
+        copy.wait()
+
+
 def kernel(
-    damping, solar, state, north, south, sides, k_lw, k_sw, daylight, cloud_top, out,
-    mix, emit, depth, factors, values,
+    damping, solar, state, north, south, west, east, k_lw, k_sw, daylight, cloud_top, out,
+    mix, sides, emit, depth, factors, values,
 ):
     fields, levels, rows, cols = state.shape
     lwb, swb = k_lw.shape[0], k_sw.shape[0]
@@ -65,6 +119,10 @@
     tops = jnp.broadcast_to(tops, (rows, cols)).astype(jnp.int32)
     days = jnp.sum(jnp.where(mine, daylight[...].astype(F32), 0.0), axis=1, keepdims=True)
     days = time_step * jnp.broadcast_to(days, (rows, cols))
+
+    for field in range(fields):
+        turned = pltpu.roll(east[field], cols - 2, 1)
+        sides[field] = jnp.where(lane % 2 == 0, west[field], turned)
 
     def damp_level(level):
         cloudy = jnp.where(level >= tops, 1.0, 0.0).astype(F32)
@@ -90,12 +148,14 @@
         cloud = cloudy.astype(BF16)
         return jnp.concatenate(highs + highs + lows + [cloud, cloud], 0)
 
-    @pl.loop(0, levels // 2)
-    def _(pair):
-        operand = jnp.concatenate([damp_level(2 * pair), damp_level(2 * pair + 1)], 1)
-        result = jnp.dot(mix[...], operand, preferred_element_type=F32)
-        depth[2 * pair] = result[:, :cols]
-        depth[2 * pair + 1] = result[:, cols:]
+    @pl.loop(0, levels // (2 * PAIRS))
+    def _(step):
+        for inner in range(PAIRS):
+            level = 2 * (PAIRS * step + inner)
+            operand = jnp.concatenate([damp_level(level), damp_level(level + 1)], 1)
+            result = jnp.dot(mix[...], operand, preferred_element_type=F32)
+            depth[level] = result[:, :cols]
+            depth[level + 1] = result[:, cols:]
 
     zero = jnp.zeros((half, cols), F32)
     log20 = math.log2(20.0)
@@ -104,32 +164,41 @@
         at = [band * rows + part * half for band in range(bands)]
         here = slice(part * half, (part + 1) * half)
 
-        def forward(level, carry):
+        def forward(level, carry, last=False):
             carry = list(carry)
             emission = emit[level, here]
-            last = jnp.where(level == levels - 1, 0.0, 1.0).astype(F32)
             for band in range(bands):
                 g, h = carry[2 * band], carry[2 * band + 1]
                 d = depth[level, at[band] : at[band] + half]
-                coupling = last * jnp.exp2(log20 - (0.1 * LOG2E) * d)
                 if band < lwb:
                     source = d * emission
                 else:
                     source = solar[band - lwb] * (1.0 - jnp.exp2(-LOG2E * d))
                 q = (1.0 + d) + g
                 w = source + h
-                r = pl.reciprocal(q + coupling, approx=True)
-                factor = coupling * r
+                if last:
+                    factor = zero
+                    r = pl.reciprocal(q, approx=True)
+                else:
+                    coupling = jnp.exp2(log20 - (0.1 * LOG2E) * d)
+                    r = pl.reciprocal(q + coupling, approx=True)
+                    factor = coupling * r
+                    carry[2 * band], carry[2 * band + 1] = factor * q, factor * w
                 factors[level, at[band] : at[band] + half] = factor
                 values[level, at[band] : at[band] + half] = w * r
-                carry[2 * band], carry[2 * band + 1] = factor * q, factor * w
             return tuple(carry)
 
-        lax.fori_loop(0, levels, forward, (zero,) * (2 * bands))
-
-        def backward(step, carry):
+        def forward_steps(step, carry):
+            for inner in range(AHEAD):
+                carry = forward(AHEAD * step + inner, carry)
+            return carry
+
+        carry = lax.fori_loop(0, levels // AHEAD - 1, forward_steps, (zero,) * (2 * bands))
+        for level in range(levels - AHEAD, levels):
+            carry = forward(level, carry, level == levels - 1)
+
+        def backward(level, carry):
             carry = list(carry)
-            level = levels - 1 - step
             emission = emit[level, here]
             lw, sw = zero, zero
             for band in range(bands):
@@ -146,31 +215,47 @@
             out[0, level, here] = out[0, level, here] + (time_step * lw + days[here] * sw)
             return tuple(carry)
 
-        lax.fori_loop(0, levels, backward, (zero,) * bands)
+        def backward_steps(step, carry):
+            for inner in range(BACK):
+                carry = backward(levels - 1 - BACK * step - inner, carry)
+            return carry
+
+        lax.fori_loop(0, levels // BACK, backward_steps, (zero,) * bands)
 
 
 def shards(state, damping, k_longwave, k_shortwave, solar, daylight, cloud_top):
     fields, levels, rows, cols = state.shape
     bands = k_longwave.shape[0] + k_shortwave.shape[0]
 
-    def ring(axis, step):
-        count = lax.axis_size(axis)
-        return [(i, (i + step) % count) for i in range(count)]
-
-    north = lax.ppermute(state[:, :, rows - 1], "gx", ring("gx", 1))
-    south = lax.ppermute(state[:, :, 0], "gx", ring("gx", -1))
-    west = lax.ppermute(jnp.swapaxes(state[:, :, :, cols - 1], 1, 2), "gy", ring("gy", 1))
-    east = lax.ppermute(jnp.swapaxes(state[:, :, :, 0], 1, 2), "gy", ring("gy", -1))
-    sides = jnp.stack([west, jnp.roll(east, -1, 2)], 3).reshape(fields, rows, 2 * levels)
     vmem = pl.BlockSpec(memory_space=pltpu.VMEM)
     smem = pl.BlockSpec(memory_space=pltpu.SMEM)
+    edge_rows = jax.ShapeDtypeStruct((fields, levels, cols), F32)
+    edge_cols = jax.ShapeDtypeStruct((fields, rows, cols), F32)
+    halos = pl.pallas_call(
+        functools.partial(exchange, (lax.axis_size("gx"), lax.axis_size("gy"))),
+        out_shape=[edge_rows, edge_rows, edge_cols, edge_cols],
+        in_specs=[vmem],
+        out_specs=[vmem] * 4,
+        scratch_shapes=[
+            pltpu.VMEM(edge_rows.shape, F32),
+            pltpu.VMEM(edge_rows.shape, F32),
+            pltpu.VMEM(edge_cols.shape, F32),
+            pltpu.SemaphoreType.DMA((4,)),
+            pltpu.SemaphoreType.DMA((4,)),
+        ],
+        compiler_params=pltpu.CompilerParams(
+            collective_id=0, has_side_effects=True, vmem_limit_bytes=8 * 1024 * 1024
+        ),
+        name="exchange",
+    )(state)
     return pl.pallas_call(
         kernel,
         out_shape=jax.ShapeDtypeStruct(state.shape, F32),
-        in_specs=[smem, smem] + [vmem] * 8,
+        in_specs=[smem, smem] + [vmem] * 9,
         out_specs=vmem,
         scratch_shapes=[
             pltpu.VMEM((bands * rows, PARTS * rows), BF16),
+            pltpu.VMEM((fields, rows, cols), F32),
             pltpu.VMEM((levels, rows, cols), F32),
             pltpu.VMEM((levels, bands * rows, cols), F32),
             pltpu.VMEM((levels, bands * rows, cols), F32),
@@ -178,7 +263,7 @@
         ],
         compiler_params=pltpu.CompilerParams(vmem_limit_bytes=48 * 1024 * 1024),
         cost_estimate=pl.CostEstimate(flops=100_000_000, bytes_accessed=4_000_000, transcendentals=5_000_000),
-    )(damping, solar, state, north, south, sides, k_longwave, k_shortwave, daylight, cloud_top)
+    )(damping, solar, state, *halos, k_longwave, k_shortwave, daylight, cloud_top)
 
 
 def solution(mesh):

time: 42.6 us -> 28.4 us (0.67)
  starting transfers between devices: 7.81 us -> 0 us
  local copies, waits for them, and re-layouts: 10.5 us -> 3.17 us
  Pallas kernels: 21.1 us -> 25 us
  waiting for transfers between devices: 2.48 us -> 0 us
    pallas_call x0 -> x1, Pallas kernels: none -> 9.98 us  [shards(): pl.pallas_call(functools.partial(exchange, (lax.axis_size('gx'), lax.axis...]
    ppermute x4 -> x0, starting transfers between devices: 7.81 us -> none  [the longest x1 5.1 us: shards(): lax.ppermute(jnp.swapaxes(state[:, :, :, 0], 1, 2), 'gy', ring('gy', -1))]
    pallas_call x1, Pallas kernels: 21.1 us -> 15 us  [shards(): pl.pallas_call(kernel, out_shape=jax.ShapeDtypeStruct(state.shape, F32),...]
    slice x3 -> x0, local copies, waits for them, and re-layouts: 5.17 us -> none  [the longest x1 4.91 us: shards(): state[:, :, :, cols - 1]]
    ppermute x4 -> x0, waiting for transfers between devices: 2.48 us -> none  [the longest x1 2.48 us: shards(): lax.ppermute(jnp.swapaxes(state[:, :, :, cols - 1], 1, 2), 'gy', ring('gy...]
    unnamed x18 -> x14, local copies, waits for them, and re-layouts: 5.09 us -> 3.17 us
  transfers between devices with their start and end apart: 4 -> 0, of which waited for: 1 -> 0; matrix products, arithmetic and copies ran while one was open for 7% -> 0% of each run, Pallas kernels for 0% -> 0%
where the time goes in v1:
time: 28.4 us; the launch traced here: 28.2 us
  Pallas kernels  25 us (88%)
  local copies, waits for them, and re-layouts  3.17 us (11%)
    pallas_call x1, Pallas kernels, shards(): pl.pallas_call(kernel, out_shape=jax.ShapeDtypeStruct(state.shape, F32),...  15 us
    pallas_call x1, Pallas kernels, shards(): pl.pallas_call(functools.partial(exchange, (lax.axis_size('gx'), lax.axis...  9.98 us
    unnamed x14, local copies, waits for them, and re-layouts  3.17 us

profile of v1, /device:TPU:0, one launch (start us, length us, event | category | flops | bytes accessed | tf_op | source)
XLA Modules:
  0.0 28.2 jit_solution(13191212429630083401)
XLA Ops:
  0.0 0.0 copy-start.5
  0.0 0.0 copy-start.4
  0.0 0.0 copy-start.3
  0.0 0.0 copy-start.2
  0.0 0.8 %copy.8.k_lw = f32[8,4]{1,0:T(8,128)S(1)} copy(f32[8,4]{0,1:T(4,128)} %param.9) | data formatting | bytes 256 | tf_op args[2]
  0.8 0.8 %copy.9.k_sw = f32[8,4]{1,0:T(8,128)S(1)} copy(f32[8,4]{0,1:T(4,128)} %param.10) | data formatting | bytes 256 | tf_op args[3]
  1.6 0.0 copy-start
  1.6 1.6 %copy-done = f32[4,64,16,128]{3,2,1,0:T(8,128)S(1)} copy-done((f32[4,64,16,128]{3,2,1,0:T(8,128)S(1)}, f32[4,64,16,128]{3,2,1,0:T(8,128)}, u32[]{:S(2)}) %copy-start) | copy-done | bytes 2097176
  3.2 0.0 copy-start.1
  3.2 10.0 %exchange.1 = (f32[4,64,128]{2,1,0:T(8,128)S(1)}, f32[4,64,128]{2,1,0:T(8,128)S(1)}, f32[4,16,128]{2,1,0:T(8,128)S(1)}, f32[4,16,128]{2,1,0:T(8,128)S(1)}) custom-call(f32[4,64,16,128]{3,2,1,0:T(8,128)S(1)} %copy-done), custom_call_target="tpu_custom_call" | custom-call | tf_op jit(solution)/shard_map/exchange/pallas_call | solution.py:234
  13.2 0.0 copy-done.5
  13.2 0.0 copy-done.4
  13.2 0.0 copy-done.3
  13.2 0.0 copy-done.2
  13.2 0.0 copy-done.1
  13.2 15.0 %shard_map.73 = f32[4,64,16,128]{3,2,1,0:T(8,128)} custom-call(f32[4,64]{1,0:T(4,128)S(1)} %copy-done.2, f32[8]{0:T(128)S(1)} %copy-done.3, f32[4,64,16,128]{3,2,1,0:T(8,128)S(1)} %copy-done.1, f32[4,64,128]{2,1,0:T(8,128)S(1)} %get-tuple-element.9.north, f32[4,64,128]{2,1,0:T(8,128)S(1)} %get-tuple-element.10.south, ...), custom_call_target="tpu_custom_call" | custom-call | flops 100000000 | bytes 4000000 | tf_op jit(solution)/shard_map/pallas_call | solution.py:251
Async XLA Ops:
  0.0 13.2 %copy-start.5 = (s32[1,128]{1,0:T(1,128)S(1)}, s32[1,128]{1,0:T(1,128)}, u32[]{:S(2)}) copy-start(s32[1,128]{1,0:T(1,128)} %cloud_top.1) | copy-start | bytes 1540
  0.0 13.2 %copy-start.4 = (s32[1,128]{1,0:T(1,128)S(1)}, s32[1,128]{1,0:T(1,128)}, u32[]{:S(2)}) copy-start(s32[1,128]{1,0:T(1,128)} %daylight.1) | copy-start | bytes 1540
  0.0 13.2 %copy-start.3 = (f32[8]{0:T(128)S(1)}, f32[8]{0:T(128)}, u32[]{:S(2)}) copy-start(f32[8]{0:T(128)} %solar.1) | copy-start | bytes 100
  0.0 13.2 %copy-start.2 = (f32[4,64]{1,0:T(4,128)S(1)}, f32[4,64]{1,0:T(4,128)}, u32[]{:S(2)}) copy-start(f32[4,64]{1,0:T(4,128)} %damping.1) | copy-start | bytes 3076
  1.6 1.6 %copy-start = (f32[4,64,16,128]{3,2,1,0:T(8,128)S(1)}, f32[4,64,16,128]{3,2,1,0:T(8,128)}, u32[]{:S(2)}) copy-start(f32[4,64,16,128]{3,2,1,0:T(8,128)} %state.3) | copy-start | bytes 6291460
  3.2 10.0 %copy-start.1 = (f32[4,64,16,128]{3,2,1,0:T(8,128)S(1)}, f32[4,64,16,128]{3,2,1,0:T(8,128)}, u32[]{:S(2)}) copy-start(f32[4,64,16,128]{3,2,1,0:T(8,128)} %state.3) | copy-start | bytes 6291460

commit v2 on v1

--- a/solution.py
+++ b/solution.py
@@ -16,7 +16,7 @@
 PARTS = 14
 
 
-PAIRS, AHEAD, BACK = 2, 4, 4
+PAIRS, AHEAD, BACK = 8, 8, 8
 
 
 def split(value):
@@ -26,16 +26,19 @@
 
 
 def build_mixing(mix, k_ref, first, cloud_depth, rows):
-    bands = k_ref.shape[0]
+    bands = k_ref.shape[1]
     width = mix.shape[1]
     group = lax.broadcasted_iota(jnp.int32, (bands, width), 1) // rows
-    k_high, k_low = split(k_ref[...])
-    k_high, k_low = k_high.astype(F32), k_low.astype(F32)
+    same = lax.broadcasted_iota(jnp.int32, (bands, bands), 0) == lax.broadcasted_iota(
+        jnp.int32, (bands, bands), 1
+    )
     cloud_high = float(np.asarray(cloud_depth, dtype=BF16))
     spread = jnp.where(group == 12, cloud_high, jnp.where(group == 13, cloud_depth - cloud_high, 0.0))
     for field in range(4):
-        high = jnp.broadcast_to(k_high[:, field : field + 1], (bands, width))
-        low = jnp.broadcast_to(k_low[:, field : field + 1], (bands, width))
+        weights = jnp.broadcast_to(k_ref[field : field + 1, :], (bands, bands))
+        weights = jnp.sum(jnp.where(same, weights, 0.0), axis=1, keepdims=True)
+        high, low = split(jnp.broadcast_to(weights, (bands, width)))
+        high, low = high.astype(F32), low.astype(F32)
         spread = jnp.where((group == field) | (group == field + 8), high, spread)
         spread = jnp.where(group == field + 4, low, spread)
     lane = lax.broadcasted_iota(jnp.int32, (rows, width), 1)
@@ -46,9 +49,15 @@
         mix[(first + band) * rows : (first + band + 1) * rows] = jnp.where(own, block, 0.0).astype(BF16)
 
 
-def exchange(shape, state, north, south, west, east, first, final, packed, send, recv):
+def exchange(
+    shape, damping, source, k_lw, k_sw, north, south, west, east, partial, mix,
+    state, first, final, packed, load, send, recv,
+):
     n_gx, n_gy = shape
-    fields, levels, rows, cols = state.shape
+    fields, levels, rows, cols = source.shape
+    loads = [pltpu.make_async_copy(source.at[field], state.at[field], load.at[field]) for field in range(fields)]
+    for copy in loads:
+        copy.start()
     gx, gy = lax.axis_index("gx"), lax.axis_index("gy")
     after, before = lax.rem(gx + 1, n_gx), lax.rem(gx + n_gx - 1, n_gx)
     right, left = lax.rem(gy + 1, n_gy), lax.rem(gy + n_gy - 1, n_gy)
@@ -58,6 +67,7 @@
     for peer in peers:
         pl.semaphore_signal(barrier, inc=1, device_id=peer, device_id_type=pl.DeviceIdType.MESH)
     for field in range(fields):
+        loads[field].wait()
         first[field] = state[field, :, 0, :]
         final[field] = state[field, :, rows - 1, :]
     pl.semaphore_wait(barrier, 4)
@@ -65,14 +75,14 @@
     moves = ((final, north), (first, south), (packed, west), (packed, east))
     copies = [
         pltpu.make_async_remote_copy(
-            src_ref=source,
+            src_ref=origin,
             dst_ref=target,
             send_sem=send.at[index],
             recv_sem=recv.at[index],
             device_id=peers[index],
             device_id_type=pl.DeviceIdType.MESH,
         )
-        for index, (source, target) in enumerate(moves)
+        for index, (origin, target) in enumerate(moves)
     ]
     copies[0].start()
     copies[1].start()
@@ -92,22 +102,39 @@
         packed[field] = held[field]
     copies[2].start()
     copies[3].start()
+
+    build_mixing(mix, k_lw, 0, 0.5, rows)
+    build_mixing(mix, k_sw, k_lw.shape[1], 0.3, rows)
+    lane = lax.broadcasted_iota(jnp.int32, (rows, cols), 1)
+    row = lax.broadcasted_iota(jnp.int32, (rows, cols), 0)
+
+    @pl.loop(0, levels // 4)
+    def _(step):
+        for inner in range(4):
+            level = 4 * step + inner
+            for field in range(fields):
+                centre = state[field, level]
+                up = jnp.where(row == 0, 0.0, pltpu.roll(centre, 1, 0))
+                down = jnp.where(row == rows - 1, 0.0, pltpu.roll(centre, rows - 1, 0))
+                before_lane = jnp.where(lane == 0, 0.0, pltpu.roll(centre, 1, 1))
+                after_lane = jnp.where(lane == cols - 1, 0.0, pltpu.roll(centre, cols - 1, 1))
+                laplace = (up + down) + (before_lane + after_lane) - 4.0 * centre
+                partial[field, level] = centre + damping[field, level] * laplace
+
     for copy in copies:
         copy.wait()
 
 
 def kernel(
-    damping, solar, state, north, south, west, east, k_lw, k_sw, daylight, cloud_top, out,
-    mix, sides, emit, depth, factors, values,
+    damping, solar, north, south, west, east, partial, mix, daylight, cloud_top, final,
+    out, sides, emit, depth, factors, values, finished,
 ):
-    fields, levels, rows, cols = state.shape
-    lwb, swb = k_lw.shape[0], k_sw.shape[0]
-    bands = lwb + swb
+    fields, levels, rows, cols = partial.shape
+    swb = solar.shape[0]
+    bands = mix.shape[0] // rows
+    lwb = bands - swb
     half = 8
     me = lax.axis_index("gx")
-
-    build_mixing(mix, k_lw, 0, 0.5, rows)
-    build_mixing(mix, k_sw, lwb, 0.3, rows)
 
     lane = lax.broadcasted_iota(jnp.int32, (rows, cols), 1)
     row = lax.broadcasted_iota(jnp.int32, (rows, cols), 0)
@@ -124,18 +151,17 @@
         turned = pltpu.roll(east[field], cols - 2, 1)
         sides[field] = jnp.where(lane % 2 == 0, west[field], turned)
 
+    border = (lane == 0) | (lane == cols - 1)
+
     def damp_level(level):
         cloudy = jnp.where(level >= tops, 1.0, 0.0).astype(F32)
         highs, lows = [], []
         for field in range(fields):
-            centre = state[field, level]
-            up = jnp.where(row == 0, north[field, pl.ds(level, 1)], pltpu.roll(centre, 1, 0))
-            down = jnp.where(row == rows - 1, south[field, pl.ds(level, 1)], pltpu.roll(centre, rows - 1, 0))
+            beside = jnp.where(row == rows - 1, south[field, pl.ds(level, 1)], 0.0)
+            beside = jnp.where(row == 0, north[field, pl.ds(level, 1)], beside)
             side = pltpu.roll(sides[field], lax.rem(cols - 2 * level, cols), 1)
-            left = jnp.where(lane == 0, side, pltpu.roll(centre, 1, 1))
-            right = jnp.where(lane == cols - 1, side, pltpu.roll(centre, cols - 1, 1))
-            laplace = (up + down) + (left + right) - 4.0 * centre
-            damped = centre + damping[field, level] * laplace
+            beside = beside + jnp.where(border, side, 0.0)
+            damped = partial[field, level] + damping[field, level] * beside
             if field == 0:
                 emit[level] = jnp.exp(0.3 * jnp.tanh(damped))
             if field == 1:
@@ -157,6 +183,8 @@
             depth[level] = result[:, :cols]
             depth[level + 1] = result[:, cols:]
 
+    stores = [pltpu.make_async_copy(out.at[pl.ds(1, fields - 1)], final.at[pl.ds(1, fields - 1)], finished.at[0])]
+    stores[0].start()
     zero = jnp.zeros((half, cols), F32)
     log20 = math.log2(20.0)
 
@@ -221,6 +249,15 @@
             return carry
 
         lax.fori_loop(0, levels // BACK, backward_steps, (zero,) * bands)
+        stores.append(
+            pltpu.make_async_copy(
+                out.at[0, :, pl.ds(part * half, half)], final.at[0, :, pl.ds(part * half, half)], finished.at[part + 1]
+            )
+        )
+        stores[-1].start()
+
+    for copy in stores:
+        copy.wait()
 
 
 def shards(state, damping, k_longwave, k_shortwave, solar, daylight, cloud_top):
@@ -231,39 +268,43 @@
     smem = pl.BlockSpec(memory_space=pltpu.SMEM)
     edge_rows = jax.ShapeDtypeStruct((fields, levels, cols), F32)
     edge_cols = jax.ShapeDtypeStruct((fields, rows, cols), F32)
+    mixing = jax.ShapeDtypeStruct((bands * rows, PARTS * rows), BF16)
     halos = pl.pallas_call(
         functools.partial(exchange, (lax.axis_size("gx"), lax.axis_size("gy"))),
-        out_shape=[edge_rows, edge_rows, edge_cols, edge_cols],
-        in_specs=[vmem],
-        out_specs=[vmem] * 4,
+        out_shape=[edge_rows, edge_rows, edge_cols, edge_cols, jax.ShapeDtypeStruct(state.shape, F32), mixing],
+        in_specs=[smem, pl.BlockSpec(memory_space=pltpu.HBM), vmem, vmem],
+        out_specs=[vmem] * 6,
         scratch_shapes=[
+            pltpu.VMEM(state.shape, F32),
             pltpu.VMEM(edge_rows.shape, F32),
             pltpu.VMEM(edge_rows.shape, F32),
             pltpu.VMEM(edge_cols.shape, F32),
+            pltpu.SemaphoreType.DMA((fields,)),
             pltpu.SemaphoreType.DMA((4,)),
             pltpu.SemaphoreType.DMA((4,)),
         ],
         compiler_params=pltpu.CompilerParams(
-            collective_id=0, has_side_effects=True, vmem_limit_bytes=8 * 1024 * 1024
+            collective_id=0, has_side_effects=True, vmem_limit_bytes=60 * 1024 * 1024
         ),
         name="exchange",
-    )(state)
+    )(damping, state, k_longwave.T, k_shortwave.T)
     return pl.pallas_call(
         kernel,
         out_shape=jax.ShapeDtypeStruct(state.shape, F32),
-        in_specs=[smem, smem] + [vmem] * 9,
-        out_specs=vmem,
+        in_specs=[smem, smem] + [vmem] * 8,
+        out_specs=pl.BlockSpec(memory_space=pl.ANY),
         scratch_shapes=[
-            pltpu.VMEM((bands * rows, PARTS * rows), BF16),
+            pltpu.VMEM(state.shape, F32),
             pltpu.VMEM((fields, rows, cols), F32),
             pltpu.VMEM((levels, rows, cols), F32),
             pltpu.VMEM((levels, bands * rows, cols), F32),
             pltpu.VMEM((levels, bands * rows, cols), F32),
             pltpu.VMEM((levels, bands * rows, cols), F32),
+            pltpu.SemaphoreType.DMA((1 + rows // 8,)),
         ],
         compiler_params=pltpu.CompilerParams(vmem_limit_bytes=48 * 1024 * 1024),
         cost_estimate=pl.CostEstimate(flops=100_000_000, bytes_accessed=4_000_000, transcendentals=5_000_000),
-    )(damping, solar, state, *halos, k_longwave, k_shortwave, daylight, cloud_top)
+    )(damping, solar, *halos, daylight, cloud_top)
 
 
 def solution(mesh):

time: 28.4 us -> 28.5 us (level)
  Pallas kernels: 25 us -> 22.3 us
  local copies, waits for them, and re-layouts: 3.17 us -> 5.82 us
    pallas_call x1, Pallas kernels: 15 us -> 9.89 us  [shards(): pl.pallas_call(kernel, out_shape=jax.ShapeDtypeStruct(state.shape, F32),...]
    unnamed x14 -> x20, local copies, waits for them, and re-layouts: 3.17 us -> 5.82 us
    pallas_call x1, Pallas kernels: 9.98 us -> 12.4 us  [shards(): pl.pallas_call(functools.partial(exchange, (lax.axis_size('gx'), lax.axis...]
where the time goes in v2:
time: 28.5 us; the launch traced here: 28.2 us
  Pallas kernels  22.3 us (78%)
  local copies, waits for them, and re-layouts  5.82 us (20%)
    pallas_call x1, Pallas kernels, shards(): pl.pallas_call(functools.partial(exchange, (lax.axis_size('gx'), lax.axis...  12.4 us
    pallas_call x1, Pallas kernels, shards(): pl.pallas_call(kernel, out_shape=jax.ShapeDtypeStruct(state.shape, F32),...  9.89 us
    unnamed x20, local copies, waits for them, and re-layouts  5.82 us

profile of v2, /device:TPU:0, one launch (start us, length us, event | category | flops | bytes accessed | tf_op | source)
XLA Modules:
  0.0 28.2 jit_solution(7690202637765253419)
XLA Ops:
  0.0 0.0 copy-start
  0.0 0.0 copy-start.9
  0.0 0.0 copy-start.8
  0.0 0.0 copy-start.7
  0.0 12.4 %exchange.1 = (f32[4,64,128]{2,1,0:T(8,128)}, f32[4,64,128]{2,1,0:T(8,128)}, f32[4,16,128]{2,1,0:T(8,128)}, f32[4,16,128]{2,1,0:T(8,128)}, f32[4,64,16,128]{3,2,1,0:T(8,128)}, /*index=5*/bf16[256,224]{1,0:T(8,128)(2,1)}) custom-call(f32[4,64]{1,0:T(4,128)} %damping.3, f32[4,64,16,128]{3,2,1,0:T(8,128)} %source.1, f32[4,8]{1,0:T(4,128)} %bitcast.2, ...), custom_call_target="tpu_custom_call" | custom-call | tf_op jit(solution)/shard_map/exchange/pallas_call | solution.py:272
  12.4 0.0 copy-done
  12.4 0.0 copy-done.9
  12.4 0.0 copy-done.8
  12.4 0.0 copy-done.7
  12.4 0.0 copy-start.1
  12.5 1.6 %copy-done.1 = f32[4,64,16,128]{3,2,1,0:T(8,128)S(1)} copy-done((f32[4,64,16,128]{3,2,1,0:T(8,128)S(1)}, f32[4,64,16,128]{3,2,1,0:T(8,128)}, u32[]{:S(2)}) %copy-start.1) | copy-done | bytes 2097176
  14.0 0.0 copy-start.2
  14.0 0.9 %copy-done.2 = f32[4,64,128]{2,1,0:T(8,128)S(1)} copy-done((f32[4,64,128]{2,1,0:T(8,128)S(1)}, f32[4,64,128]{2,1,0:T(8,128)}, u32[]{:S(2)}) %copy-start.2) | copy-done | bytes 131096
  14.9 0.0 copy-start.3
  14.9 0.9 %copy-done.3 = f32[4,64,128]{2,1,0:T(8,128)S(1)} copy-done((f32[4,64,128]{2,1,0:T(8,128)S(1)}, f32[4,64,128]{2,1,0:T(8,128)}, u32[]{:S(2)}) %copy-start.3) | copy-done | bytes 131096
  15.8 0.0 copy-start.4
  15.8 0.9 %copy-done.4 = bf16[256,224]{1,0:T(8,128)(2,1)S(1)} copy-done((bf16[256,224]{1,0:T(8,128)(2,1)S(1)}, bf16[256,224]{1,0:T(8,128)(2,1)}, u32[]{:S(2)}) %copy-start.4) | copy-done | bytes 114712
  16.8 0.0 copy-start.5
  16.8 0.8 %copy-done.5 = f32[4,16,128]{2,1,0:T(8,128)S(1)} copy-done((f32[4,16,128]{2,1,0:T(8,128)S(1)}, f32[4,16,128]{2,1,0:T(8,128)}, u32[]{:S(2)}) %copy-start.5) | copy-done | bytes 32792
  17.5 0.0 copy-start.6
  17.5 0.8 %copy-done.6 = f32[4,16,128]{2,1,0:T(8,128)S(1)} copy-done((f32[4,16,128]{2,1,0:T(8,128)S(1)}, f32[4,16,128]{2,1,0:T(8,128)}, u32[]{:S(2)}) %copy-start.6) | copy-done | bytes 32792
  18.3 9.9 %shard_map.73 = f32[4,64,16,128]{3,2,1,0:T(8,128)} custom-call(f32[4,64]{1,0:T(4,128)S(1)} %copy-done, f32[8]{0:T(128)S(1)} %copy-done.7, f32[4,64,128]{2,1,0:T(8,128)S(1)} %copy-done.2, f32[4,64,128]{2,1,0:T(8,128)S(1)} %copy-done.3, f32[4,16,128]{2,1,0:T(8,128)S(1)} %copy-done.5, f32[4,16,128]{2,1,0:T(8,128)S(1)} %copy-done.6, ...), custom_call_target="tpu_custom_call" | custom-call | flops 100000000 | bytes 4000000 | tf_op jit(solution)/shard_map/pallas_call | solution.py:291
Async XLA Ops:
  0.0 12.4 %copy-start = (f32[4,64]{1,0:T(4,128)S(1)}, f32[4,64]{1,0:T(4,128)}, u32[]{:S(2)}) copy-start(f32[4,64]{1,0:T(4,128)} %damping.3) | copy-start | bytes 3076
  0.0 12.4 %copy-start.9 = (s32[1,128]{1,0:T(1,128)S(1)}, s32[1,128]{1,0:T(1,128)}, u32[]{:S(2)}) copy-start(s32[1,128]{1,0:T(1,128)} %cloud_top.1) | copy-start | bytes 1540
  0.0 12.4 %copy-start.8 = (s32[1,128]{1,0:T(1,128)S(1)}, s32[1,128]{1,0:T(1,128)}, u32[]{:S(2)}) copy-start(s32[1,128]{1,0:T(1,128)} %daylight.1) | copy-start | bytes 1540
  0.0 12.4 %copy-start.7 = (f32[8]{0:T(128)S(1)}, f32[8]{0:T(128)}, u32[]{:S(2)}) copy-start(f32[8]{0:T(128)} %solar.1) | copy-start | bytes 100
  12.4 1.6 %copy-start.1 = (f32[4,64,16,128]{3,2,1,0:T(8,128)S(1)}, f32[4,64,16,128]{3,2,1,0:T(8,128)}, u32[]{:S(2)}) copy-start(f32[4,64,16,128]{3,2,1,0:T(8,128)} %get-tuple-element.15.partial) | copy-start | bytes 6291460
  14.0 0.9 %copy-start.2 = (f32[4,64,128]{2,1,0:T(8,128)S(1)}, f32[4,64,128]{2,1,0:T(8,128)}, u32[]{:S(2)}) copy-start(f32[4,64,128]{2,1,0:T(8,128)} %get-tuple-element.11.north) | copy-start | bytes 393220
  14.9 0.9 %copy-start.3 = (f32[4,64,128]{2,1,0:T(8,128)S(1)}, f32[4,64,128]{2,1,0:T(8,128)}, u32[]{:S(2)}) copy-start(f32[4,64,128]{2,1,0:T(8,128)} %get-tuple-element.12.south) | copy-start | bytes 393220
  15.8 0.9 %copy-start.4 = (bf16[256,224]{1,0:T(8,128)(2,1)S(1)}, bf16[256,224]{1,0:T(8,128)(2,1)}, u32[]{:S(2)}) copy-start(bf16[256,224]{1,0:T(8,128)(2,1)} %get-tuple-element.16.mix) | copy-start | bytes 344068
  16.8 0.8 %copy-start.5 = (f32[4,16,128]{2,1,0:T(8,128)S(1)}, f32[4,16,128]{2,1,0:T(8,128)}, u32[]{:S(2)}) copy-start(f32[4,16,128]{2,1,0:T(8,128)} %get-tuple-element.13.west) | copy-start | bytes 98308
  17.5 0.8 %copy-start.6 = (f32[4,16,128]{2,1,0:T(8,128)S(1)}, f32[4,16,128]{2,1,0:T(8,128)}, u32[]{:S(2)}) copy-start(f32[4,16,128]{2,1,0:T(8,128)} %get-tuple-element.14.east) | copy-start | bytes 98308

commit v3 on v2

--- a/solution.py
+++ b/solution.py
@@ -284,7 +284,7 @@
             pltpu.SemaphoreType.DMA((4,)),
         ],
         compiler_params=pltpu.CompilerParams(
-            collective_id=0, has_side_effects=True, vmem_limit_bytes=60 * 1024 * 1024
+            collective_id=0, has_side_effects=True, vmem_limit_bytes=51 * 1024 * 1024
         ),
         name="exchange",
     )(damping, state, k_longwave.T, k_shortwave.T)

time: 28.5 us -> 22.8 us (0.80)
  local copies, waits for them, and re-layouts: 5.82 us -> 2.1 us
  Pallas kernels: 22.3 us -> 20.5 us
    unnamed x20 -> x12, local copies, waits for them, and re-layouts: 5.82 us -> 2.1 us
    pallas_call x1, Pallas kernels: 12.4 us -> 10.6 us  [shards(): pl.pallas_call(functools.partial(exchange, (lax.axis_size('gx'), lax.axis...]
where the time goes in v3:
time: 22.8 us; the launch traced here: 22.6 us
  Pallas kernels  20.5 us (90%)
  local copies, waits for them, and re-layouts  2.1 us (9%)
    pallas_call x1, Pallas kernels, shards(): pl.pallas_call(functools.partial(exchange, (lax.axis_size('gx'), lax.axis...  10.6 us
    pallas_call x1, Pallas kernels, shards(): pl.pallas_call(kernel, out_shape=jax.ShapeDtypeStruct(state.shape, F32),...  9.86 us
    unnamed x12, local copies, waits for them, and re-layouts  2.1 us

profile of v3, /device:TPU:0, one launch (start us, length us, event | category | flops | bytes accessed | tf_op | source)
XLA Modules:
  0.0 22.6 jit_solution(7928142013919786705)
XLA Ops:
  0.0 0.0 copy-start.5
  0.0 0.0 copy-start.4
  0.0 0.0 copy-start.3
  0.0 0.0 copy-start
  0.0 0.7 %copy-done = f32[8,4]{0,1:T(4,128)S(1)} copy-done((f32[8,4]{0,1:T(4,128)S(1)}, f32[8,4]{0,1:T(4,128)}, u32[]{:S(2)}) %copy-start) | copy-done | bytes 152
  0.7 0.0 copy-start.1
  0.7 0.7 %copy-done.1 = f32[8,4]{0,1:T(4,128)S(1)} copy-done((f32[8,4]{0,1:T(4,128)S(1)}, f32[8,4]{0,1:T(4,128)}, u32[]{:S(2)}) %copy-start.1) | copy-done | bytes 152
  1.4 0.0 copy-start.2
  1.4 0.7 %copy-done.2 = f32[4,64]{1,0:T(4,128)S(1)} copy-done((f32[4,64]{1,0:T(4,128)S(1)}, f32[4,64]{1,0:T(4,128)}, u32[]{:S(2)}) %copy-start.2) | copy-done | bytes 1048
  2.1 10.6 %exchange.1 = (f32[4,64,128]{2,1,0:T(8,128)S(1)}, f32[4,64,128]{2,1,0:T(8,128)S(1)}, f32[4,16,128]{2,1,0:T(8,128)S(1)}, f32[4,16,128]{2,1,0:T(8,128)S(1)}, f32[4...) custom-call(f32[4,64]{1,0:T(4,128)S(1)} %copy-done.2, f32[4,64,16,128]{3,2,1,0:T(8,128)} %source.1, ...), custom_call_target="tpu_custom_call" | custom-call | tf_op jit(solution)/shard_map/exchange/pallas_call | solution.py:272
  12.7 0.0 copy-done.5
  12.7 0.0 copy-done.4
  12.7 0.0 copy-done.3
  12.7 9.9 %shard_map.73 = f32[4,64,16,128]{3,2,1,0:T(8,128)} custom-call(f32[4,64]{1,0:T(4,128)S(1)} %copy-done.2, f32[8]{0:T(128)S(1)} %copy-done.3, f32[4,64,128]{2,1,0:T(8,128)S(1)} %get-tuple-element.11.north, f32[4,64,128]{2,1,0:T(8,128)S(1)} %get-tuple-element.12.south, f32[4,16,128]{2,1,0:T(8,128)S(1)} %get-tuple-element.13.west, ...), custom_call_target="tpu_custom_call" | custom-call | flops 100000000 | bytes 4000000 | tf_op jit(solution)/shard_map/pallas_call | solution.py:291
Async XLA Ops:
  0.0 12.7 %copy-start.5 = (s32[1,128]{1,0:T(1,128)S(1)}, s32[1,128]{1,0:T(1,128)}, u32[]{:S(2)}) copy-start(s32[1,128]{1,0:T(1,128)} %cloud_top.1) | copy-start | bytes 1540
  0.0 12.7 %copy-start.4 = (s32[1,128]{1,0:T(1,128)S(1)}, s32[1,128]{1,0:T(1,128)}, u32[]{:S(2)}) copy-start(s32[1,128]{1,0:T(1,128)} %daylight.1) | copy-start | bytes 1540
  0.0 12.7 %copy-start.3 = (f32[8]{0:T(128)S(1)}, f32[8]{0:T(128)}, u32[]{:S(2)}) copy-start(f32[8]{0:T(128)} %solar.1) | copy-start | bytes 100
  0.0 0.7 %copy-start = (f32[8,4]{0,1:T(4,128)S(1)}, f32[8,4]{0,1:T(4,128)}, u32[]{:S(2)}) copy-start(f32[8,4]{0,1:T(4,128)} %param.9) | copy-start | bytes 388
  0.7 0.7 %copy-start.1 = (f32[8,4]{0,1:T(4,128)S(1)}, f32[8,4]{0,1:T(4,128)}, u32[]{:S(2)}) copy-start(f32[8,4]{0,1:T(4,128)} %param.10) | copy-start | bytes 388
  1.4 0.7 %copy-start.2 = (f32[4,64]{1,0:T(4,128)S(1)}, f32[4,64]{1,0:T(4,128)}, u32[]{:S(2)}) copy-start(f32[4,64]{1,0:T(4,128)} %damping.3) | copy-start | bytes 3076

commit v4 on v3

--- a/solution.py
+++ b/solution.py
@@ -16,7 +16,7 @@
 PARTS = 14
 
 
-PAIRS, AHEAD, BACK = 8, 8, 8
+PAIRS, AHEAD, BACK = 16, 16, 16
 
 
 def split(value):
@@ -50,7 +50,7 @@
 
 
 def exchange(
-    shape, damping, source, k_lw, k_sw, north, south, west, east, partial, mix,
+    shape, damping, source, north, south, west, east, partial,
     state, first, final, packed, load, send, recv,
 ):
     n_gx, n_gy = shape
@@ -103,8 +103,6 @@
     copies[2].start()
     copies[3].start()
 
-    build_mixing(mix, k_lw, 0, 0.5, rows)
-    build_mixing(mix, k_sw, k_lw.shape[1], 0.3, rows)
     lane = lax.broadcasted_iota(jnp.int32, (rows, cols), 1)
     row = lax.broadcasted_iota(jnp.int32, (rows, cols), 0)
 
@@ -126,16 +124,17 @@
 
 
 def kernel(
-    damping, solar, north, south, west, east, partial, mix, daylight, cloud_top, final,
-    out, sides, emit, depth, factors, values, finished,
+    damping, solar, north, south, west, east, partial, k_lw, k_sw, daylight, cloud_top, final,
+    out, mix, sides, emit, depth, factors, values, finished,
 ):
     fields, levels, rows, cols = partial.shape
-    swb = solar.shape[0]
-    bands = mix.shape[0] // rows
-    lwb = bands - swb
+    lwb, swb = k_lw.shape[1], k_sw.shape[1]
+    bands = lwb + swb
     half = 8
     me = lax.axis_index("gx")
 
+    build_mixing(mix, k_lw, 0, 0.5, rows)
+    build_mixing(mix, k_sw, lwb, 0.3, rows)
     lane = lax.broadcasted_iota(jnp.int32, (rows, cols), 1)
     row = lax.broadcasted_iota(jnp.int32, (rows, cols), 0)
     total = cloud_top.shape[1]
@@ -268,12 +267,11 @@
     smem = pl.BlockSpec(memory_space=pltpu.SMEM)
     edge_rows = jax.ShapeDtypeStruct((fields, levels, cols), F32)
     edge_cols = jax.ShapeDtypeStruct((fields, rows, cols), F32)
-    mixing = jax.ShapeDtypeStruct((bands * rows, PARTS * rows), BF16)
     halos = pl.pallas_call(
         functools.partial(exchange, (lax.axis_size("gx"), lax.axis_size("gy"))),
-        out_shape=[edge_rows, edge_rows, edge_cols, edge_cols, jax.ShapeDtypeStruct(state.shape, F32), mixing],
-        in_specs=[smem, pl.BlockSpec(memory_space=pltpu.HBM), vmem, vmem],
-        out_specs=[vmem] * 6,
+        out_shape=[edge_rows, edge_rows, edge_cols, edge_cols, jax.ShapeDtypeStruct(state.shape, F32)],
+        in_specs=[smem, pl.BlockSpec(memory_space=pltpu.HBM)],
+        out_specs=[vmem] * 5,
         scratch_shapes=[
             pltpu.VMEM(state.shape, F32),
             pltpu.VMEM(edge_rows.shape, F32),
@@ -287,14 +285,15 @@
             collective_id=0, has_side_effects=True, vmem_limit_bytes=51 * 1024 * 1024
         ),
         name="exchange",
-    )(damping, state, k_longwave.T, k_shortwave.T)
+    )(damping, state)
     return pl.pallas_call(
         kernel,
         out_shape=jax.ShapeDtypeStruct(state.shape, F32),
-        in_specs=[smem, smem] + [vmem] * 8,
+        in_specs=[smem, smem] + [vmem] * 9,
         out_specs=pl.BlockSpec(memory_space=pl.ANY),
         scratch_shapes=[
             pltpu.VMEM(state.shape, F32),
+            pltpu.VMEM((bands * rows, PARTS * rows), BF16),
             pltpu.VMEM((fields, rows, cols), F32),
             pltpu.VMEM((levels, rows, cols), F32),
             pltpu.VMEM((levels, bands * rows, cols), F32),
@@ -304,7 +303,7 @@
         ],
         compiler_params=pltpu.CompilerParams(vmem_limit_bytes=48 * 1024 * 1024),
         cost_estimate=pl.CostEstimate(flops=100_000_000, bytes_accessed=4_000_000, transcendentals=5_000_000),
-    )(damping, solar, *halos, daylight, cloud_top)
+    )(damping, solar, *halos, k_longwave.T, k_shortwave.T, daylight, cloud_top)
 
 
 def solution(mesh):

time: 22.8 us -> 20.8 us (0.912)
  local copies, waits for them, and re-layouts: 2.1 us -> 0.75 us
  Pallas kernels: 20.5 us -> 19.8 us
    unnamed x12, local copies, waits for them, and re-layouts: 2.1 us -> 0.75 us
    pallas_call x1, Pallas kernels: 9.86 us -> 9.22 us  [shards(): pl.pallas_call(kernel, out_shape=jax.ShapeDtypeStruct(state.shape, F32),...]
where the time goes in v4:
time: 20.8 us; the launch traced here: 20.6 us
  Pallas kernels  19.8 us (95%)
  local copies, waits for them, and re-layouts  0.75 us (4%)
    pallas_call x1, Pallas kernels, shards(): pl.pallas_call(functools.partial(exchange, (lax.axis_size('gx'), lax.axis...  10.6 us
    pallas_call x1, Pallas kernels, shards(): pl.pallas_call(kernel, out_shape=jax.ShapeDtypeStruct(state.shape, F32),...  9.22 us
    unnamed x12, local copies, waits for them, and re-layouts  0.75 us

profile of v4, /device:TPU:0, one launch (start us, length us, event | category | flops | bytes accessed | tf_op | source)
XLA Modules:
  0.0 20.6 jit_solution(9241082496325585701)
XLA Ops:
  0.0 0.0 copy-start.5
  0.0 0.0 copy-start.4
  0.0 0.0 copy-start.3
  0.0 0.0 copy-start.1
  0.0 0.0 copy-start
  0.0 0.7 %copy-done = f32[4,64]{1,0:T(4,128)S(1)} copy-done((f32[4,64]{1,0:T(4,128)S(1)}, f32[4,64]{1,0:T(4,128)}, u32[]{:S(2)}) %copy-start) | copy-done | bytes 1048
  0.7 0.0 copy-start.2
  0.7 10.6 %exchange.1 = (f32[4,64,128]{2,1,0:T(8,128)S(1)}, f32[4,64,128]{2,1,0:T(8,128)S(1)}, f32[4,16,128]{2,1,0:T(8,128)S(1)}, f32[4,16,128]{2,1,0:T(8,128)S(1)}, f32[4,64,16,128]{3,2,1,0:T(8,128)S(1)}) custom-call(f32[4,64]{1,0:T(4,128)S(1)} %copy-done, f32[4,64,16,128]{3,2,1,0:T(8,128)} %source.1), custom_call_target="tpu_custom_call" | custom-call | tf_op jit(solution)/shard_map/exchange/pallas_call | solution.py:270
  11.4 0.0 copy-done.5
  11.4 0.0 copy-done.4
  11.4 0.0 copy-done.3
  11.4 0.0 copy-done.1
  11.4 0.0 copy-done.2
  11.4 9.2 %shard_map.73 = f32[4,64,16,128]{3,2,1,0:T(8,128)} custom-call(f32[4,64]{1,0:T(4,128)S(1)} %copy-done, f32[8]{0:T(128)S(1)} %copy-done.3, f32[4,64,128]{2,1,0:T(8,128)S(1)} %get-tuple-element.10.north, f32[4,64,128]{2,1,0:T(8,128)S(1)} %get-tuple-element.11.south, f32[4,16,128]{2,1,0:T(8,128)S(1)} %get-tuple-element.12.west, ...), custom_call_target="tpu_custom_call" | custom-call | flops 100000000 | bytes 4000000 | tf_op jit(solution)/shard_map/pallas_call | solution.py:289
Async XLA Ops:
  0.0 11.4 %copy-start.5 = (s32[1,128]{1,0:T(1,128)S(1)}, s32[1,128]{1,0:T(1,128)}, u32[]{:S(2)}) copy-start(s32[1,128]{1,0:T(1,128)} %cloud_top.1) | copy-start | bytes 1540
  0.0 11.4 %copy-start.4 = (s32[1,128]{1,0:T(1,128)S(1)}, s32[1,128]{1,0:T(1,128)}, u32[]{:S(2)}) copy-start(s32[1,128]{1,0:T(1,128)} %daylight.1) | copy-start | bytes 1540
  0.0 11.4 %copy-start.3 = (f32[8]{0:T(128)S(1)}, f32[8]{0:T(128)}, u32[]{:S(2)}) copy-start(f32[8]{0:T(128)} %solar.1) | copy-start | bytes 100
  0.0 11.4 %copy-start.1 = (f32[8,4]{0,1:T(4,128)S(1)}, f32[8,4]{0,1:T(4,128)}, u32[]{:S(2)}) copy-start(f32[8,4]{0,1:T(4,128)} %param.9) | copy-start | bytes 388
  0.0 0.7 %copy-start = (f32[4,64]{1,0:T(4,128)S(1)}, f32[4,64]{1,0:T(4,128)}, u32[]{:S(2)}) copy-start(f32[4,64]{1,0:T(4,128)} %damping.3) | copy-start | bytes 3076
  0.7 10.7 %copy-start.2 = (f32[8,4]{0,1:T(4,128)S(1)}, f32[8,4]{0,1:T(4,128)}, u32[]{:S(2)}) copy-start(f32[8,4]{0,1:T(4,128)} %param.10) | copy-start | bytes 388
